TPU v7x, 32 devices: a whole 2x2x4 slice. The times are simulated.
32 devices in a mesh: shard: 4 (over x, core), rep: 8 (over z, y).
Axes of the slice: x: 2, y: 2, z: 4, core: 2. Of those that a mesh axis runs over, the one named last changes fastest.
Arguments:
- tokens: bfloat16 [32768, 576], P(('shard', 'rep')), may hold values from -6 to 6
- cotangent: bfloat16 [32768, 576], P(('shard', 'rep')), may hold values from -6 to 6
- segment_ids: int32 [32768], P(('shard', 'rep')), may hold values from 0 to 16, as said below
- current_attention: bfloat16 [576], replicated, may hold values from 0.5 to 1.5
- current_project: bfloat16 [576, 960], replicated, may hold values from -0.25 to 0.25
- current_output: bfloat16 [576, 576], replicated, may hold values from -2.5 to 2.5
- current_feeding: bfloat16 [576], replicated, may hold values from 0.5 to 1.5
- current_gating: bfloat16 [576, 1536], replicated, may hold values from -0.25 to 0.25
- current_upward: bfloat16 [576, 1536], replicated, may hold values from -0.25 to 0.25
- current_downward: bfloat16 [1536, 576], replicated, may hold values from -0.15625 to 0.15625
- master_attention: float32 [576], P('shard'), may hold values from 0.5 to 1.5
- master_project: float32 [576, 960], P('shard'), may hold values from -0.25 to 0.25
- master_output: float32 [576, 576], P('shard'), may hold values from -2.5 to 2.5
- master_feeding: float32 [576], P('shard'), may hold values from 0.5 to 1.5
- master_gating: float32 [576, 1536], P('shard'), may hold values from -0.25 to 0.25
- master_upward: float32 [576, 1536], P('shard'), may hold values from -0.25 to 0.25
- master_downward: float32 [1536, 576], P('shard'), may hold values from -0.15625 to 0.15625
- momentum_attention: float32 [576], P('shard'), may hold values from -0.046875 to 0.046875
- momentum_project: float32 [576, 960], P('shard'), may hold values from -0.046875 to 0.046875
- momentum_output: float32 [576, 576], P('shard'), may hold values from -0.00390625 to 0.00390625
- momentum_feeding: float32 [576], P('shard'), may hold values from -0.0078125 to 0.0078125
- momentum_gating: float32 [576, 1536], P('shard'), may hold values from -0.00390625 to 0.00390625
- momentum_upward: float32 [576, 1536], P('shard'), may hold values from -0.00390625 to 0.00390625
- momentum_downward: float32 [1536, 576], P('shard'), may hold values from -0.005859375 to 0.005859375
- variance_attention: float32 [576], P('shard'), may hold values from 7.324219e-05 to 0.0007324219
- variance_project: float32 [576, 960], P('shard'), may hold values from 7.324219e-05 to 0.0007324219
- variance_output: float32 [576, 576], P('shard'), may hold values from 4.882813e-07 to 4.8828124e-06
- variance_feeding: float32 [576], P('shard'), may hold values from 1.953125e-06 to 1.953125e-05
- variance_gating: float32 [576, 1536], P('shard'), may hold values from 4.882813e-07 to 4.8828124e-06
- variance_upward: float32 [576, 1536], P('shard'), may hold values from 4.882813e-07 to 4.8828124e-06
- variance_downward: float32 [1536, 576], P('shard'), may hold values from 1.0986328e-06 to 1.0986329e-05
Outputs:
- block_output: bfloat16 [32768, 576], P(('shard', 'rep'))
- tokens_gradient: bfloat16 [32768, 576], P(('shard', 'rep'))
- gradient_attention: float32 [576], P('shard')
- gradient_project: float32 [576, 960], P('shard')
- gradient_output: float32 [576, 576], P('shard')
- gradient_feeding: float32 [576], P('shard')
- gradient_gating: float32 [576, 1536], P('shard')
- gradient_upward: float32 [576, 1536], P('shard')
- gradient_downward: float32 [1536, 576], P('shard')
- updated_attention: float32 [576], P('shard')
- updated_project: float32 [576, 960], P('shard')
- updated_output: float32 [576, 576], P('shard')
- updated_feeding: float32 [576], P('shard')
- updated_gating: float32 [576, 1536], P('shard')
- updated_upward: float32 [576, 1536], P('shard')
- updated_downward: float32 [1536, 576], P('shard')
- velocity_attention: float32 [576], P('shard')
- velocity_project: float32 [576, 960], P('shard')
- velocity_output: float32 [576, 576], P('shard')
- velocity_feeding: float32 [576], P('shard')
- velocity_gating: float32 [576, 1536], P('shard')
- velocity_upward: float32 [576, 1536], P('shard')
- velocity_downward: float32 [1536, 576], P('shard')
- spread_attention: float32 [576], P('shard')
- spread_project: float32 [576, 960], P('shard')
- spread_output: float32 [576, 576], P('shard')
- spread_feeding: float32 [576], P('shard')
- spread_gating: float32 [576, 1536], P('shard')
- spread_upward: float32 [576, 1536], P('shard')
- spread_downward: float32 [1536, 576], P('shard')
- rounded_attention: bfloat16 [576], replicated
- rounded_project: bfloat16 [576, 960], replicated
- rounded_output: bfloat16 [576, 576], replicated
- rounded_feeding: bfloat16 [576], replicated
- rounded_gating: bfloat16 [576, 1536], replicated
- rounded_upward: bfloat16 [576, 1536], replicated
- rounded_downward: bfloat16 [1536, 576], replicated
Inputs may be any that keep to these rules, and one draw needn't show every extreme that they name: `segment_ids`: within each sequence of 1024 rows the segment ids start at 0 and rise by one at each new document; every document has at least 60 tokens.
All inputs are finite; a program needn't handle non-finite values.
Results may differ from a plain program's by a relative error of at most 0.013.
Values may be sent and summed in bfloat16 or wider, within the bound.
A program may use at most 192 MiB of HBM per device.

v0:
```python
import math

import jax
import jax.numpy as jnp
from jax import lax
from jax.sharding import PartitionSpec as P

D = 576
H = 9
KV = 3
HS = 64
FF = 1536
STEP = 5


EPSILON = 1e-05
THETA = 10000.0
BETA = 0.5
ADAM_EPSILON = 1e-08
DECAY = 0.1
NEGATIVE = -1e30
BASE_RATE = 0.3


def positions_of(segment):
    places = jnp.arange(segment.shape[0], dtype=jnp.int32)
    before = jnp.concatenate([segment[:1] - 1, segment[:-1]])
    starts = jnp.where(segment != before, places, 0)
    return places - lax.cummax(starts, axis=0)


def rope_tables(segment):
    half_size = HS // 2
    places = positions_of(segment).astype(jnp.float32)
    frequency = jnp.exp(jnp.arange(half_size, dtype=jnp.float32) * (-2.0 * math.log(THETA) / HS))
    angles = places[:, None] * frequency[None, :]
    return (jnp.cos(angles), jnp.sin(angles))


def rotate(values, cosine_table, sine_table):
    half_size = values.shape[-1] // 2
    first_half = values[..., :half_size]
    second_half = values[..., half_size:]
    return jnp.concatenate(
        [
            first_half * cosine_table - second_half * sine_table,
            second_half * cosine_table + first_half * sine_table,
        ],
        axis=-1,
    )


def unrotate(values, cosine_table, sine_table):
    half_size = values.shape[-1] // 2
    first_half = values[..., :half_size]
    second_half = values[..., half_size:]
    return jnp.concatenate(
        [
            first_half * cosine_table + second_half * sine_table,
            second_half * cosine_table - first_half * sine_table,
        ],
        axis=-1,
    )


def gram_product(left, right):
    return lax.dot_general(
        left, right, (((0,), (0,)), ((), ())), preferred_element_type=jnp.float32
    )


def back_product(left, right):
    return lax.dot_general(
        left, right, (((1,), (1,)), ((), ())), preferred_element_type=jnp.float32
    )


def rate_scales():
    return (
        1.0,
        float(D) ** (-0.5),
        float(max(D // 96, 1)) ** (-0.5),
        1.0,
        float(D) ** (-0.5),
        float(D) ** (-0.5),
        float(FF) ** (-0.5),
    )


def body(
    tokens,
    cotangent,
    segment_ids,
    current_attention,
    current_project,
    current_output,
    current_feeding,
    current_gating,
    current_upward,
    current_downward,
    master_attention,
    master_project,
    master_output,
    master_feeding,
    master_gating,
    master_upward,
    master_downward,
    momentum_attention,
    momentum_project,
    momentum_output,
    momentum_feeding,
    momentum_gating,
    momentum_upward,
    momentum_downward,
    variance_attention,
    variance_project,
    variance_output,
    variance_feeding,
    variance_gating,
    variance_upward,
    variance_downward,
):
    rows_count = tokens.shape[0]
    group_size = H // KV
    score_scale = 1.0 / math.sqrt(HS)
    block_rows = min(512, rows_count)
    inputs_float = tokens.astype(jnp.float32)
    gain_one = current_attention.astype(jnp.float32)
    scale_one = lax.rsqrt(jnp.mean(inputs_float * inputs_float, axis=-1, keepdims=True) + EPSILON)
    unit_one = inputs_float * scale_one
    normed = (unit_one * gain_one).astype(jnp.bfloat16)
    joined = jnp.dot(normed, current_project, preferred_element_type=jnp.float32)
    cosine_table, sine_table = rope_tables(segment_ids)
    cosine_query = cosine_table[:, None, None, :]
    sine_query = sine_table[:, None, None, :]
    cosine_key = cosine_table[:, None, :]
    sine_key = sine_table[:, None, :]
    queries = rotate(
        joined[:, : H * HS].reshape(rows_count, KV, group_size, HS), cosine_query, sine_query
    ).astype(jnp.bfloat16)
    key_rows = rotate(
        joined[:, H * HS : (H + KV) * HS].reshape(rows_count, KV, HS), cosine_key, sine_key
    ).astype(jnp.bfloat16)
    value_rows = joined[:, (H + KV) * HS :].reshape(rows_count, KV, HS).astype(jnp.bfloat16)
    places = jnp.arange(rows_count)

    def block_scores(first_row, last_row):
        scores = (
            jnp.einsum(
                "qngd,knd->ngqk",
                queries[first_row:last_row],
                key_rows[:last_row],
                preferred_element_type=jnp.float32,
            )
            * score_scale
        )
        allowed = (segment_ids[first_row:last_row, None] == segment_ids[None, :last_row]) & (
            places[first_row:last_row, None] >= places[None, :last_row]
        )
        return (scores, allowed)

    mixed_parts = []
    log_totals = []
    for first_row in range(0, rows_count, block_rows):
        last_row = first_row + block_rows
        scores, allowed = block_scores(first_row, last_row)
        masked = jnp.where(allowed, scores, NEGATIVE)
        row_peak = jnp.max(masked, axis=-1, keepdims=True)
        exponents = jnp.exp(masked - row_peak)
        row_total = jnp.sum(exponents, axis=-1, keepdims=True)
        weights = (exponents / row_total).astype(jnp.bfloat16)
        mixed_block = jnp.einsum(
            "ngqk,knd->qngd", weights, value_rows[:last_row], preferred_element_type=jnp.float32
        )
        mixed_parts.append(mixed_block.reshape(block_rows, H * HS))
        log_totals.append(row_peak + jnp.log(row_total))
    mixed_rows = jnp.concatenate(mixed_parts, axis=0).astype(jnp.bfloat16)
    residual = inputs_float + jnp.dot(
        mixed_rows, current_output, preferred_element_type=jnp.float32
    )
    gain_two = current_feeding.astype(jnp.float32)
    scale_two = lax.rsqrt(jnp.mean(residual * residual, axis=-1, keepdims=True) + EPSILON)
    unit_two = residual * scale_two
    normed_two = (unit_two * gain_two).astype(jnp.bfloat16)
    gate_values = jnp.dot(normed_two, current_gating, preferred_element_type=jnp.float32)
    up_values = jnp.dot(normed_two, current_upward, preferred_element_type=jnp.float32)
    hidden = (jax.nn.silu(gate_values) * up_values).astype(jnp.bfloat16)
    outputs = residual + jnp.dot(hidden, current_downward, preferred_element_type=jnp.float32)
    block_output = outputs.astype(jnp.bfloat16)
    grad_outputs = cotangent.astype(jnp.float32)
    grad_downward = gram_product(hidden, cotangent)
    grad_hidden = back_product(cotangent, current_downward)
    sigmoid_gate = jax.nn.sigmoid(gate_values)
    grad_gate = (
        grad_hidden * up_values * sigmoid_gate * (1.0 + gate_values * (1.0 - sigmoid_gate))
    ).astype(jnp.bfloat16)
    grad_up = (grad_hidden * gate_values * sigmoid_gate).astype(jnp.bfloat16)
    grad_gating = gram_product(normed_two, grad_gate)
    grad_upward = gram_product(normed_two, grad_up)
    grad_normed_two = back_product(grad_gate, current_gating) + back_product(
        grad_up, current_upward
    )
    grad_feeding = jnp.sum(grad_normed_two * unit_two, axis=0)
    grad_unit_two = grad_normed_two * gain_two
    grad_residual = grad_outputs + scale_two * (
        grad_unit_two - unit_two * jnp.mean(grad_unit_two * unit_two, axis=-1, keepdims=True)
    )
    grad_attended = grad_residual.astype(jnp.bfloat16)
    grad_output = gram_product(mixed_rows, grad_attended)
    grad_mixed = (
        back_product(grad_attended, current_output)
        .astype(jnp.bfloat16)
        .reshape(rows_count, KV, group_size, HS)
    )
    query_parts = []
    grad_keys = jnp.zeros((rows_count, KV, HS), jnp.float32)
    grad_values = jnp.zeros((rows_count, KV, HS), jnp.float32)
    for block_number, first_row in enumerate(range(0, rows_count, block_rows)):
        last_row = first_row + block_rows
        scores, allowed = block_scores(first_row, last_row)
        probability = jnp.where(allowed, jnp.exp(scores - log_totals[block_number]), 0.0)
        grad_block = grad_mixed[first_row:last_row]
        grad_weights = jnp.einsum(
            "qngd,knd->ngqk", grad_block, value_rows[:last_row], preferred_element_type=jnp.float32
        )
        centre = jnp.sum(probability * grad_weights, axis=-1, keepdims=True)
        grad_scores = (probability * (grad_weights - centre)).astype(jnp.bfloat16)
        padding = ((0, rows_count - last_row), (0, 0), (0, 0))
        value_term = jnp.einsum(
            "ngqk,qngd->knd",
            probability.astype(jnp.bfloat16),
            grad_block,
            preferred_element_type=jnp.float32,
        )
        grad_values = grad_values + jnp.pad(value_term, padding)
        key_term = (
            jnp.einsum(
                "ngqk,qngd->knd",
                grad_scores,
                queries[first_row:last_row],
                preferred_element_type=jnp.float32,
            )
            * score_scale
        )
        grad_keys = grad_keys + jnp.pad(key_term, padding)
        query_parts.append(
            jnp.einsum(
                "ngqk,knd->qngd",
                grad_scores,
                key_rows[:last_row],
                preferred_element_type=jnp.float32,
            )
            * score_scale
        )
    grad_queries = unrotate(jnp.concatenate(query_parts, axis=0), cosine_query, sine_query)
    grad_keys = unrotate(grad_keys, cosine_key, sine_key)
    grad_joined = jnp.concatenate(
        [
            grad_queries.reshape(rows_count, H * HS),
            grad_keys.reshape(rows_count, KV * HS),
            grad_values.reshape(rows_count, KV * HS),
        ],
        axis=1,
    ).astype(jnp.bfloat16)
    grad_project = gram_product(normed, grad_joined)
    grad_normed = back_product(grad_joined, current_project)
    grad_attention = jnp.sum(grad_normed * unit_one, axis=0)
    grad_unit_one = grad_normed * gain_one
    grad_tokens = grad_residual + scale_one * (
        grad_unit_one - unit_one * jnp.mean(grad_unit_one * unit_one, axis=-1, keepdims=True)
    )
    tokens_gradient = grad_tokens.astype(jnp.bfloat16)
    shard_size = lax.axis_size("shard")
    total_rows = rows_count * shard_size * lax.axis_size("rep")
    summed = lax.psum(
        (
            grad_attention,
            grad_project,
            grad_output,
            grad_feeding,
            grad_gating,
            grad_upward,
            grad_downward,
        ),
        ("shard", "rep"),
    )
    shard_index = lax.axis_index("shard")
    summed = tuple(
        (
            lax.dynamic_slice_in_dim(
                whole_sum,
                shard_index * (whole_sum.shape[0] // shard_size),
                whole_sum.shape[0] // shard_size,
                0,
            )
            for whole_sum in summed
        )
    )
    gradients = tuple((whole_sum / total_rows for whole_sum in summed))
    masters = (
        master_attention,
        master_project,
        master_output,
        master_feeding,
        master_gating,
        master_upward,
        master_downward,
    )
    moments = (
        momentum_attention,
        momentum_project,
        momentum_output,
        momentum_feeding,
        momentum_gating,
        momentum_upward,
        momentum_downward,
    )
    variances = (
        variance_attention,
        variance_project,
        variance_output,
        variance_feeding,
        variance_gating,
        variance_upward,
        variance_downward,
    )
    scales = rate_scales()
    correction = 1.0 - BETA**STEP
    velocities = []
    spreads = []
    updates = []
    for number in range(7):
        grad_value = gradients[number]
        rate = BASE_RATE * scales[number]
        velocity = BETA * moments[number] + (1.0 - BETA) * grad_value
        spread = BETA * variances[number] + (1.0 - BETA) * grad_value * grad_value
        direction = velocity / correction / (jnp.sqrt(spread / correction) + ADAM_EPSILON)
        if number in (0, 3):
            updated = masters[number] - rate * direction
        else:
            updated = masters[number] - rate * (direction + DECAY * masters[number])
        velocities.append(velocity)
        spreads.append(spread)
        updates.append(updated)
    rounded = (
        lax.all_gather(updates[0].astype(jnp.bfloat16), "shard", axis=0, tiled=True),
        lax.all_gather(updates[1].astype(jnp.bfloat16), "shard", axis=0, tiled=True),
        lax.all_gather(updates[2].astype(jnp.bfloat16), "shard", axis=0, tiled=True),
        lax.all_gather(updates[3].astype(jnp.bfloat16), "shard", axis=0, tiled=True),
        lax.all_gather(updates[4].astype(jnp.bfloat16), "shard", axis=0, tiled=True),
        lax.all_gather(updates[5].astype(jnp.bfloat16), "shard", axis=0, tiled=True),
        lax.all_gather(updates[6].astype(jnp.bfloat16), "shard", axis=0, tiled=True),
    )
    return (
        block_output,
        tokens_gradient,
        gradients[0],
        gradients[1],
        gradients[2],
        gradients[3],
        gradients[4],
        gradients[5],
        gradients[6],
        updates[0],
        updates[1],
        updates[2],
        updates[3],
        updates[4],
        updates[5],
        updates[6],
        velocities[0],
        velocities[1],
        velocities[2],
        velocities[3],
        velocities[4],
        velocities[5],
        velocities[6],
        spreads[0],
        spreads[1],
        spreads[2],
        spreads[3],
        spreads[4],
        spreads[5],
        spreads[6],
        rounded[0],
        rounded[1],
        rounded[2],
        rounded[3],
        rounded[4],
        rounded[5],
        rounded[6],
    )


def solution(mesh):
    in_specs = (
        P(("shard", "rep"), None),
        P(("shard", "rep"), None),
        P(("shard", "rep")),
        P(),
        P(),
        P(),
        P(),
        P(),
        P(),
        P(),
        P("shard"),
        P("shard", None),
        P("shard", None),
        P("shard"),
        P("shard", None),
        P("shard", None),
        P("shard", None),
        P("shard"),
        P("shard", None),
        P("shard", None),
        P("shard"),
        P("shard", None),
        P("shard", None),
        P("shard", None),
        P("shard"),
        P("shard", None),
        P("shard", None),
        P("shard"),
        P("shard", None),
        P("shard", None),
        P("shard", None),
    )
    out_specs = (
        P(("shard", "rep"), None),
        P(("shard", "rep"), None),
        P("shard"),
        P("shard", None),
        P("shard", None),
        P("shard"),
        P("shard", None),
        P("shard", None),
        P("shard", None),
        P("shard"),
        P("shard", None),
        P("shard", None),
        P("shard"),
        P("shard", None),
        P("shard", None),
        P("shard", None),
        P("shard"),
        P("shard", None),
        P("shard", None),
        P("shard"),
        P("shard", None),
        P("shard", None),
        P("shard", None),
        P("shard"),
        P("shard", None),
        P("shard", None),
        P("shard"),
        P("shard", None),
        P("shard", None),
        P("shard", None),
        P(),
        P(),
        P(),
        P(),
        P(),
        P(),
        P(),
    )
    return jax.shard_map(body, mesh=mesh, in_specs=in_specs, out_specs=out_specs, check_vma=False)
```

profile of v0, /device:TPU:1, one launch (start us, length us, event | category | flops | bytes accessed | tf_op | source)
XLA Modules:
  0.0 538.4 jit_solution(2036625934503418662)
XLA Ops:
  27.3 3.7 fusion.40
  31.5 8.0 %fusion.5 = (f32[3,3,512]{2,1,0:T(4,128)S(1)}, f32[3,1024,512,3]{2,1,3,0:T(8,128)}) fusion(pred[512,1024]{0,1:T(8,128)(4,1)S(1)} %fusion.36, bf16[1024,3,3,32]{0,3,2,1:T(8,128)(2,1)S(1)} %get-tuple-element.91, bf16[1024,3,3,32]{0,3,2,1:T(8,128)(2,1)S(1)} %get-tuple-element.90, bf16[1024,3,32]{0,2,1:T(8,128)(2,1)S(1)} %get-tuple-element.97, ...), kind=kOutput, calls=%fused_computation.11 | convolution fusion | flops 620097024 | bytes 20989952 | tf_op jit(solution)/shard_map/qngd,knd->ngqk/dot_general | solution.py:149
  39.6 10.2 %fusion.6 = f32[3,3,512]{2,1,0:T(4,128)S(1)} fusion(f32[3,1024,512,3]{2,1,3,0:T(8,128)} %get-tuple-element.105, f32[3,3,512]{2,1,0:T(4,128)S(1)} %get-tuple-element.104, pred[512,1024]{0,1:T(8,128)(4,1)S(1)} %fusion.36), kind=kLoop, calls=%fused_computation.12 | loop fusion | flops 18869760 | bytes 19435520 | tf_op jit(solution)/shard_map/reduce_sum | solution.py:170
  50.4 9.6 %fusion.39 = bf16[3,64,3,512]{3,1,2,0:T(8,128)(2,1)S(1)} fusion(bf16[1024,3,64,1]{0,2,3,1:T(8,128)(2,1)} %bitcast.205, f32[3,1024,512,3]{2,1,3,0:T(8,128)} %get-tuple-element.105, f32[3,3,512]{2,1,0:T(4,128)} %copy-done.37, f32[3,3,512]{2,1,0:T(4,128)S(1)} %get-tuple-element.104, pred[512,1024]{0,1:T(8,128)(4,1)S(1)} %fusion.36), kind=kOutput, calls=%fused_computation.70 | convolution fusion | flops 627867648 | bytes 20418560 | tf_op jit(solution)/shard_map/ngqk,knd->qngd/dot_general | solution.py:172
  66.3 4.6 fusion.107
  70.9 8.7 %multiply_convert_fusion = (bf16[1024,1536]{1,0:T(8,128)(2,1)S(1)}, bf16[1024,1536]{1,0:T(8,128)(2,1)S(1)}, bf16[1024,1536]{1,0:T(8,128)(2,1)}) fusion(f32[1024,1536]{1,0:T(8,128)} %fusion.107, f32[1024,1536]{1,0:T(8,128)S(1)} %fusion.108, bf16[1024,576]{0,1:T(8,128)(2,1)S(1)} %copy-done.26, bf16[1536,576]{0,1:T(8,128)(2,1)S(1)} %copy-done), kind=kOutput, calls=%fused_computation.30 | convolution fusion | flops 1837105152 | bytes 24969216 | tf_op jit(solution)/shard_map/dot_general | solution.py:73
  81.6 3.8 fusion.110
  85.4 3.8 fusion.111
  99.4 5.8 %fusion.8 = (f32[3,3,512]{2,1,0:T(4,128)S(1)}, f32[3,512,512,3]{2,1,3,0:T(8,128)}) fusion(f32[3,512,512,3]{2,1,3,0:T(8,128)S(1)} %bitcast.198, f32[3,3,512]{2,1,0:T(4,128)S(1)} %log_add_fusion.1, pred[512,512]{0,1:T(8,128)(4,1)S(1)} %copy-done.6, bf16[512,3,64,1]{0,2,3,1:T(8,128)(2,1)S(1)} %bitcast.210, bf16[512,3,3,64]{0,3,2,1:T(8,128)(2,1)S(1)} %bitcast.202), kind=kOutput, calls=%fused_computation.16 | convolution fusion | flops 313781760 | bytes 19959808 | tf_op jit(solution)/shard_map/qngd,knd->ngqk/dot_general | solution.py:223
  105.2 11.3 %fusion.10 = bf16[3,3,512,512]{2,3,1,0:T(8,128)(2,1)} fusion(f32[3,512,512,3]{2,1,3,0:T(8,128)} %get-tuple-element.114, f32[3,512,512,3]{2,1,3,0:T(8,128)} %copy-done.1, f32[3,3,512]{2,1,0:T(4,128)S(1)} %get-tuple-element.113, f32[3,3,512]{2,1,0:T(4,128)S(1)} %log_add_fusion.1, pred[512,512]{0,1:T(8,128)(4,1)} %copy-done.5), kind=kLoop, calls=%fused_computation.18 | loop fusion | flops 14155776 | bytes 23891968 | tf_op jit(solution)/shard_map/convert_element_type | solution.py:227
  116.4 4.2 fusion.57
  122.9 3.7 fusion.112
  126.7 13.1 %fusion = (f32[3,3,512]{2,1,0:T(4,128)S(1)}, f32[3,1024,512,3]{2,1,3,0:T(8,128)}) fusion(f32[3,1024,512,3]{2,1,3,0:T(8,128)} %get-tuple-element.105, f32[3,3,512]{2,1,0:T(4,128)S(1)} %log_add_fusion, pred[512,1024]{0,1:T(8,128)(4,1)S(1)} %fusion.36, bf16[1024,3,64,1]{0,2,3,1:T(8,128)(2,1)S(1)} %bitcast.206, bf16[512,3,3,64]{0,3,2,1:T(8,128)(2,1)S(1)} %bitcast.203), kind=kOutput, calls=%fused_computation.2 | convolution fusion | flops 627568128 | bytes 39292928 | tf_op jit(solution)/shard_map/qngd,knd->ngqk/dot_general | solution.py:223
  139.8 8.4 %fusion.50 = bf16[1024,3,64]{0,2,1:T(8,128)(2,1)S(1)} fusion(bf16[512,3,3,64]{0,3,2,1:T(8,128)(2,1)S(1)} %bitcast.204, f32[3,1024,512,3]{2,1,3,0:T(8,128)} %get-tuple-element.105, f32[3,3,512]{2,1,0:T(4,128)S(1)} %log_add_fusion, pred[512,1024]{0,1:T(8,128)(4,1)S(1)} %fusion.36, f32[512,3,64]{0,2,1:T(8,128)S(1)} %copy-done.55), kind=kOutput, calls=%fused_computation.78 | convolution fusion | flops 623247360 | bytes 20793344 | tf_op jit(solution)/shard_map/ngqk,qngd->knd/dot_general | solution.py:229
  148.2 13.8 %fusion.2 = bf16[3,3,512,1024]{2,3,1,0:T(8,128)(2,1)S(1)} fusion(f32[3,1024,512,3]{2,1,3,0:T(8,128)} %get-tuple-element.112, f32[3,1024,512,3]{2,1,3,0:T(8,128)} %get-tuple-element.105, f32[3,3,512]{2,1,0:T(4,128)S(1)} %get-tuple-element.111, f32[3,3,512]{2,1,0:T(4,128)S(1)} %log_add_fusion, pred[512,1024]{0,1:T(8,128)(4,1)S(1)} %fusion.36), kind=kLoop, calls=%fused_computation.4 | loop fusion | flops 28311552 | bytes 47747072 | tf_op jit(solution)/shard_map/convert_element_type | solution.py:227
  171.4 258.5 %all-reduce.9.cloned.1.call-done = (f32[576,960]{1,0:T(8,128)}, f32[576,576]{1,0:T(8,128)}, f32[576,1536]{1,0:T(8,128)}, f32[576,1536]{1,0:T(8,128)}, f32[1536,576]{0,1:T(8,128)}) async-done(((f32[576,960]{1,0:T(8,128)}, f32[576,576]{1,0:T(8,128)}, f32[576,1536]{1,0:T(8,128)}, f32[576,1536]{1,0:T(8,128)}, f32[1536,576]{0,1:T(8,128)}), (f32[576,960]{1,0:T(8,128)}, f32[576,576]{1,0:T(8,128)}, ...) | async-done | bytes 14155792 | tf_op jit(solution)/shard_map/psum | solution.py:275
  433.4 4.4 fusion.97
  437.9 4.5 fusion.99
  442.5 4.4 fusion.98
  448.3 4.7 fusion.34
  453.0 39.7 %all-reduce.4 = (f32[576]{0:T(1024)S(1)}, f32[576]{0:T(1024)S(1)}) all-reduce(f32[576]{0:T(1024)S(1)} %get-tuple-element.39, f32[576]{0:T(1024)S(1)} %get-tuple-element.37), channel_id=1, replica_groups=mesh['shard'=4,'rep'=8] {'shard','rep'}, use_global_device_ids=true, to_apply=%region_13.14 | all-reduce | flops 1152 | bytes 9216 | tf_op jit(solution)/shard_map/psum | solution.py:275
  493.8 7.2 %all-reduce.6 = (bf16[576]{0:T(1024)(128)(2,1)}, bf16[576]{0:T(1024)(128)(2,1)}) all-reduce(bf16[576]{0:T(1024)(128)(2,1)S(1)} %dynamic-update-slice, bf16[576]{0:T(1024)(128)(2,1)S(1)} %dynamic-update-slice.1), channel_id=1, replica_groups=mesh['shard'=4,'rep'=8] {'shard'}, use_global_device_ids=true, to_apply=%add.2 | all-reduce | flops 1152 | bytes 4608
  501.0 4.1 fusion.33
  510.5 12.6 %all_gather.23 = bf16[576,576]{1,0:T(8,128)(2,1)S(1)} all-gather(bf16[144,576]{1,0:T(8,128)(2,1)S(1)} %get-tuple-element.65), channel_id=1, replica_groups=mesh['shard'=4,'rep'=8] {'shard'}, dimensions={0}, use_global_device_ids=true | all-gather | bytes 829440 | tf_op jit(solution)/shard_map/all_gather | solution.py:348
  (199 shorter events, 69.1 us)
Async XLA Ops:
  7.2 63.7 %copy-start = (bf16[1536,576]{0,1:T(8,128)(2,1)S(1)}, bf16[1536,576]{0,1:T(8,128)(2,1)}, u32[]{:S(2)}) copy-start(bf16[1536,576]{0,1:T(8,128)(2,1)} %param.40) | copy-start | bytes 5308420
  7.2 422.7 %all-reduce.9.cloned.1.call-start = ((), (), s32[]{:S(2)}) async-start(), calls=%async_computation.4 | async-start | bytes 28901376 | tf_op jit(solution)/shard_map/psum | solution.py:275
  15.1 10.6 %copy-start.29 = (bf16[512,192]{0,1:T(8,128)(2,1)}, bf16[512,192]{0,1:T(8,128)(2,1)S(1)}, u32[]{:S(2)}) copy-start(bf16[512,192]{0,1:T(8,128)(2,1)S(1)} %slice.130) | copy-start | bytes 589828
  21.6 9.9 %copy-start.9 = (bf16[1024,3,3,32]{0,3,2,1:T(8,128)(2,1)}, bf16[1024,3,3,32]{0,3,2,1:T(8,128)(2,1)S(1)}, u32[]{:S(2)}) copy-start(bf16[1024,3,3,32]{0,3,2,1:T(8,128)(2,1)S(1)} %get-tuple-element.90) | copy-start | bytes 1769476
  21.6 9.9 %copy-start.11 = (bf16[1024,3,3,32]{0,3,2,1:T(8,128)(2,1)}, bf16[1024,3,3,32]{0,3,2,1:T(8,128)(2,1)S(1)}, u32[]{:S(2)}) copy-start(bf16[1024,3,3,32]{0,3,2,1:T(8,128)(2,1)S(1)} %get-tuple-element.91) | copy-start | bytes 1769476
  21.8 9.7 %copy-start.21 = (bf16[1024,3,32]{0,2,1:T(8,128)(2,1)}, bf16[1024,3,32]{0,2,1:T(8,128)(2,1)S(1)}, u32[]{:S(2)}) copy-start(bf16[1024,3,32]{0,2,1:T(8,128)(2,1)S(1)} %get-tuple-element.96) | copy-start | bytes 589828
  21.8 9.7 %copy-start.23 = (bf16[1024,3,32]{0,2,1:T(8,128)(2,1)}, bf16[1024,3,32]{0,2,1:T(8,128)(2,1)S(1)}, u32[]{:S(2)}) copy-start(bf16[1024,3,32]{0,2,1:T(8,128)(2,1)S(1)} %get-tuple-element.97) | copy-start | bytes 589828
  50.4 9.7 %copy-start.4 = (bf16[1024,576]{0,1:T(8,128)(2,1)S(1)}, bf16[1024,576]{0,1:T(8,128)(2,1)}, u32[]{:S(2)}) copy-start(bf16[1024,576]{0,1:T(8,128)(2,1)} %param.31) | copy-start | bytes 3538948
  50.4 9.7 %copy-start.31 = (bf16[3,64,3,512]{3,1,2,0:T(8,128)(2,1)S(1)}, bf16[3,64,3,512]{3,1,2,0:T(8,128)(2,1)}, u32[]{:S(2)}) copy-start(bf16[3,64,3,512]{3,1,2,0:T(8,128)(2,1)} %fusion.40) | copy-start | bytes 1769476
  50.4 9.7 %copy-start.50 = (bf16[576,576]{1,0:T(8,128)(2,1)S(1)}, bf16[576,576]{1,0:T(8,128)(2,1)}, u32[]{:S(2)}) copy-start(bf16[576,576]{1,0:T(8,128)(2,1)} %param.36) | copy-start | bytes 1990660
  61.2 30.4 %copy-start.7 = (f32[1024,576]{0,1:T(8,128)}, f32[1024,576]{0,1:T(8,128)S(1)}, u32[]{:S(2)}) copy-start(f32[1024,576]{0,1:T(8,128)S(1)} %get-tuple-element.109) | copy-start | bytes 7077892
  89.2 7.4 %slice-start.1 = ((s8[9437184]{0:T(1024)(128)(4,1)}), s8[4194304]{0:T(1024)(128)(4,1)S(1)}, s32[]{:S(2)}) async-start(s8[9437184]{0:T(1024)(128)(4,1)} %bitcast.197), calls=%async_computation.6 | async-start | bytes 8388608
  126.7 13.1 %copy-start.55 = (f32[512,3,64]{0,2,1:T(8,128)S(1)}, f32[512,3,64]{0,2,1:T(8,128)}, u32[]{:S(2)}) copy-start(f32[512,3,64]{0,2,1:T(8,128)} %fusion.53) | copy-start | bytes 1179652
  148.2 19.3 %copy-start.51 = (bf16[1024,3,64]{0,2,1:T(8,128)(2,1)}, bf16[1024,3,64]{0,2,1:T(8,128)(2,1)S(1)}, u32[]{:S(2)}) copy-start(bf16[1024,3,64]{0,2,1:T(8,128)(2,1)S(1)} %fusion.50) | copy-start | bytes 1179652
  171.3 351.8 %all-gather.5.cloned.1.call-start = ((), (), s32[]{:S(2)}) async-start(), calls=%async_computation | async-start | bytes 1474560 | tf_op jit(solution)/shard_map/all_gather | solution.py:347
  433.4 89.8 %all-gather.11.cloned.1.call-start = ((), (), s32[]{:S(2)}) async-start(), calls=%async_computation.3 | async-start | bytes 2211840 | tf_op jit(solution)/shard_map/all_gather | solution.py:352
  437.8 85.3 %all-gather.7.cloned.1.call-start = ((), (), s32[]{:S(2)}) async-start(), calls=%async_computation.1 | async-start | bytes 2211840 | tf_op jit(solution)/shard_map/all_gather | solution.py:350
  442.4 81.0 %all-gather.9.cloned.1.call-start = ((), (), s32[]{:S(2)}) async-start(), calls=%async_computation.2 | async-start | bytes 2211840 | tf_op jit(solution)/shard_map/all_gather | solution.py:351
  448.2 44.5 %copy-start.42 = (f32[144]{0:T(256)S(1)}, f32[144]{0:T(256)}, u32[]{:S(2)}) copy-start(f32[144]{0:T(256)} %param.44) | copy-start | bytes 1732
  448.2 44.5 %copy-start.43 = (f32[144]{0:T(256)S(1)}, f32[144]{0:T(256)}, u32[]{:S(2)}) copy-start(f32[144]{0:T(256)} %param.51) | copy-start | bytes 1732
  448.2 44.5 %copy-start.44 = (f32[144]{0:T(256)S(1)}, f32[144]{0:T(256)}, u32[]{:S(2)}) copy-start(f32[144]{0:T(256)} %param.58) | copy-start | bytes 1732
  448.2 44.5 %copy-start.45 = (f32[144]{0:T(256)S(1)}, f32[144]{0:T(256)}, u32[]{:S(2)}) copy-start(f32[144]{0:T(256)} %param.41) | copy-start | bytes 1732
  448.2 44.5 %copy-start.46 = (f32[144]{0:T(256)S(1)}, f32[144]{0:T(256)}, u32[]{:S(2)}) copy-start(f32[144]{0:T(256)} %param.55) | copy-start | bytes 1732
  448.2 44.5 %copy-start.47 = (f32[144]{0:T(256)S(1)}, f32[144]{0:T(256)}, u32[]{:S(2)}) copy-start(f32[144]{0:T(256)} %param.48) | copy-start | bytes 1732
  (40 other events, 119.7 us)
Sparse Core Ops, SparseCore 0:
  171.4 258.4 all-reduce.8
  433.5 16.9 all-gather.4
  452.6 20.9 all-gather.10
  475.5 21.3 all-gather.6
  498.9 24.4 all-gather.8
where the time goes:
time: 545 us; the launch traced here: 538 us
  waiting for transfers between devices  259 us (48%)
  matrix products  113 us (21%)
  other arithmetic  68.8 us (13%)
  blocking collectives  59.5 us (11%)
  local copies, waits for them, and re-layouts  21.4 us (4%)
  between operations  16.4 us (3%)
    psum x1, waiting for transfers between devices, body(): lax.psum((grad_attention, grad_project, grad_output, grad_feeding, grad_g...  259 us
    psum x1, blocking collectives, body(): lax.psum((grad_attention, grad_project, grad_output, grad_feeding, grad_g...  39.7 us
    convert_element_type x2, other arithmetic, body(): grad_scores = (probability * (grad_weights - centre)).astype(jnp.bfloat16)  25.1 us
    dot_general x5, matrix products, back_product(): lax.dot_general(left, right, (((1,), (1,)), ((), ())), preferred_element_...  19 us
    dot_general x2, matrix products, body(): jnp.einsum('qngd,knd->ngqk', grad_block, value_rows[:last_row], preferred...  18.8 us
    dot_general x5, matrix products, gram_product(): lax.dot_general(left, right, (((0,), (0,)), ((), ())), preferred_element_...  16.4 us
    unnamed x128, local copies, waits for them, and re-layouts  15.8 us
    dot_general x2, matrix products, body(): jnp.einsum('ngqk,knd->qngd', weights, value_rows[:last_row], preferred_el...  13.3 us
  transfers between devices with their start and end apart: 5, of which 2 were waited for; matrix products, arithmetic and copies ran while one was open for 5% of the time, Pallas kernels for 0%

commit v1 on v0

v1 whole, which is shorter than its diff:
```python
import math

import jax
import jax.numpy as jnp
from jax import lax
from jax.experimental import pallas as pl
from jax.experimental.pallas import tpu as pltpu
from jax.sharding import PartitionSpec as P

D = 576
H = 9
KV = 3
HS = 64
FF = 1536
QKV = 960
STEP = 5
GROUP = H // KV

EPSILON = 1e-05
THETA = 10000.0
BETA = 0.5
ADAM_EPSILON = 1e-08
DECAY = 0.1
NEGATIVE = -1e30
BASE_RATE = 0.3

F32 = jnp.float32
BF16 = jnp.bfloat16
T = 256
PR = D // 4
PC = FF // 4


def dot(a, b):
    return jnp.dot(a, b, preferred_element_type=F32)


def dot_t(a, b):
    return lax.dot_general(a, b, (((1,), (1,)), ((), ())), preferred_element_type=F32)


def column(ref, size):
    row = jnp.broadcast_to(ref[...].astype(F32).reshape(1, size), (8, size))
    return row.T[:, :1]


def block_kernel(
    xt_ref, ct_ref, seg_ref, g1_ref, g2_ref, wp_ref, wo_ref, wg_ref, wu_ref, wdt_ref,
    bot_ref, tgt_ref, gain_ref, gr_ref,
    qt, kt_, vt, kn, vn, nt, mt, gmt, et, eb, invl, gres, dgain,
):
    rows = xt_ref.shape[1]
    tiles = rows // T
    half = HS // 2

    seg_row = seg_ref[...].astype(F32)
    seg_cols = jnp.broadcast_to(seg_row, (8, rows)).T[:, :1]
    starts = jnp.zeros((1, rows), F32)
    for k in range(0, rows, 128):
        lower = (seg_cols[k : k + 128] < seg_row).astype(F32)
        starts = starts + jnp.sum(lower, axis=0, keepdims=True)
    places_row = lax.broadcasted_iota(jnp.int32, (1, rows), 1).astype(F32)
    index = lax.broadcasted_iota(jnp.int32, (half, 1), 0).astype(F32)
    frequency = jnp.exp(index * (-2.0 * math.log(THETA) / HS))
    angles = frequency * (places_row - starts)
    cosine = jnp.cos(angles)
    sine = jnp.sin(angles)

    gain1 = column(g1_ref, D)
    gain2 = column(g2_ref, D)
    dgain[...] = jnp.zeros_like(dgain)

    def unit_one(cols):
        xf = xt_ref[:, cols].astype(F32)
        scale = lax.rsqrt(jnp.mean(xf * xf, axis=0, keepdims=True) + EPSILON)
        return xf * scale, scale

    def project(wpt):
        wpt[...] = wp_ref[...].T
        for r in range(tiles):
            r0 = r * T
            cs = cosine[:, r0 : r0 + T]
            sn = sine[:, r0 : r0 + T]
            unit, _ = unit_one(slice(r0, r0 + T))
            normed = (unit * gain1).astype(BF16)
            nt[:, r0 : r0 + T] = normed
            joined = dot(wpt[...], normed)
            for h in range(H + 2 * KV):
                jt = joined[h * HS : (h + 1) * HS]
                a = jt[:half]
                b = jt[half:]
                if h < H:
                    qt[h, 0:half, r0 : r0 + T] = ((a * cs - b * sn) * (HS**-0.5)).astype(BF16)
                    qt[h, half:HS, r0 : r0 + T] = ((b * cs + a * sn) * (HS**-0.5)).astype(BF16)
                elif h < H + KV:
                    kt_[h - H, 0:half, r0 : r0 + T] = (a * cs - b * sn).astype(BF16)
                    kt_[h - H, half:HS, r0 : r0 + T] = (b * cs + a * sn).astype(BF16)
                else:
                    vt[h - H - KV, :, r0 : r0 + T] = jt.astype(BF16)

    pl.run_scoped(project, pltpu.VMEM((QKV, D), BF16))
    for n in range(KV):
        kn[n] = kt_[n].T
        vn[n] = vt[n].T

    def ef(k, i):
        if k < 2:
            return et, k * T, i * T
        return eb, (k - 2) * T, (i - 2) * T

    def forward(bias, sc):
        for i in range(tiles):
            for k in range(i + 1):
                kk = lax.broadcasted_iota(jnp.int32, (T, T), 0).astype(F32) + float(k * T)
                ok = kk >= starts[:, i * T : (i + 1) * T]
                if k == i:
                    qq = lax.broadcasted_iota(jnp.int32, (T, T), 1).astype(F32) + float(i * T)
                    ok = ok & (kk <= qq)
                bias[i * (i + 1) // 2 + k] = jnp.where(ok, 0.0, NEGATIVE)

        def head(h, _):
            n = h // GROUP
            for i in range(tiles):
                q = qt[h, :, i * T : (i + 1) * T]
                peak = None
                for k in range(i + 1):
                    s = dot(kn[n, k * T : (k + 1) * T, :], q) + bias[i * (i + 1) // 2 + k]
                    sc[i % 2, k] = s
                    top = jnp.max(s, axis=0, keepdims=True)
                    peak = top if peak is None else jnp.maximum(peak, top)
                total = jnp.zeros((1, T), F32)
                out = jnp.zeros((HS, T), F32)
                for k in range(i + 1):
                    e = jnp.exp(sc[i % 2, k] - peak)
                    total = total + jnp.sum(e, axis=0, keepdims=True)
                    e16 = e.astype(BF16)
                    ref, a, b = ef(k, i)
                    ref[h, a : a + T, b : b + T] = e16
                    out = out + dot(vt[n, :, k * T : (k + 1) * T], e16)
                inverse = 1.0 / total
                invl[h, :, i * T : (i + 1) * T] = inverse
                mt[pl.ds(pl.multiple_of(h * HS, HS), HS), i * T : (i + 1) * T] = (
                    out * inverse
                ).astype(BF16)
            return 0

        lax.fori_loop(0, H, head, 0)

    pl.run_scoped(
        forward,
        pltpu.VMEM((tiles * (tiles + 1) // 2, T, T), F32),
        pltpu.VMEM((2, tiles, T, T), F32),
    )

    RT = 512
    CT = 256

    def feeding(wot, cn, n2, n2t, hid, gg, gu, res):
        wot[...] = wo_ref[...].T
        cn[...] = ct_ref[...].T

        def rowtile(r, _):
            rs = pl.ds(pl.multiple_of(r * RT, RT), RT)
            residual = xt_ref[:, rs].astype(F32) + dot(wot[...], mt[:, rs])
            scale = lax.rsqrt(jnp.mean(residual * residual, axis=0, keepdims=True) + EPSILON)
            res[...] = residual
            n2v = (residual * scale * gain2).astype(BF16)
            n2t[:, rs] = n2v
            n2[...] = n2v.T

            def col(j, _):
                js = pl.ds(pl.multiple_of(j * CT, CT), CT)
                gate = dot(n2[...], wg_ref[:, js])
                up = dot(n2[...], wu_ref[:, js])
                gh = dot(cn[rs, :], wdt_ref[:, js])
                sg = 0.5 * jnp.tanh(0.5 * gate) + 0.5
                sl = gate * sg
                hid[rs, js] = (sl * up).astype(BF16)
                gg[rs, js] = (gh * up * (sg + sl * (1.0 - sg))).astype(BF16)
                gu[rs, js] = (gh * sl).astype(BF16)
                return 0

            lax.fori_loop(0, FF // CT, col, 0)
            residual = res[...]
            bot_ref[:, rs] = (residual + dot_t(wdt_ref[...], hid[rs, :])).astype(BF16)
            gn2 = dot_t(wg_ref[...], gg[rs, :]) + dot_t(wu_ref[...], gu[rs, :])
            unit = residual * scale
            dgain[:, 1:2] += jnp.sum(gn2 * unit, axis=1, keepdims=True)
            e = gn2 * gain2
            gr = ct_ref[:, rs].astype(F32) + scale * (
                e - unit * jnp.mean(e * unit, axis=0, keepdims=True)
            )
            gres[:, rs] = gr
            gmt[:, rs] = dot(wo_ref[...], gr.astype(BF16)).astype(BF16)
            return 0

        lax.fori_loop(0, rows // RT, rowtile, 0)

        def wide(j, _):
            js = pl.ds(pl.multiple_of(j * PC, PC), PC)
            gr_ref[2, j] = dot(ct_ref[...], hid[:, js]).astype(BF16).reshape(4, PR, PC)
            gr_ref[0, :, j] = dot(n2t[...], gg[:, js]).astype(BF16).reshape(4, PR, PC)
            gr_ref[1, :, j] = dot(n2t[...], gu[:, js]).astype(BF16).reshape(4, PR, PC)
            return 0

        lax.fori_loop(0, FF // PC, wide, 0)
        gr_ref[3, :, 3] = dot_t(mt[...], gres[:PC].astype(BF16)).astype(BF16).reshape(4, PR, PC)
        part = dot_t(mt[...], gres[PC:].astype(BF16)).astype(BF16)
        gr_ref[3, :, 2, :, PC // 2 :] = part.reshape(4, PR, PC // 2)

    pl.run_scoped(
        feeding,
        pltpu.VMEM((D, D), BF16),
        pltpu.VMEM((rows, D), BF16),
        pltpu.VMEM((RT, D), BF16),
        pltpu.VMEM((D, rows), BF16),
        pltpu.VMEM((rows, FF), BF16),
        pltpu.VMEM((rows, FF), BF16),
        pltpu.VMEM((rows, FF), BF16),
        pltpu.VMEM((D, RT), F32),
    )

    def backward(ds, gjt, dk, dv, cs_ref, sn_ref):
        cs_ref[...] = cosine
        sn_ref[...] = sine

        def unrotate(v, base):
            a = v[:half]
            b = v[half:]
            cs = cs_ref[...]
            sn = sn_ref[...]
            gjt[pl.ds(pl.multiple_of(base, HS), half), :] = (a * cs + b * sn).astype(BF16)
            gjt[pl.ds(pl.multiple_of(base + half, half), half), :] = (b * cs - a * sn).astype(BF16)

        def head(h, _):
            n = h // GROUP
            hs = pl.ds(pl.multiple_of(h * HS, HS), HS)
            first = lax.rem(h, GROUP) == 0

            @pl.when(first)
            def _():
                dk[...] = jnp.zeros_like(dk)
                dv[...] = jnp.zeros_like(dv)

            do = (gmt[hs, :].astype(F32) * invl[h]).astype(BF16)
            delta = jnp.sum(do.astype(F32) * mt[hs, :].astype(F32), axis=0, keepdims=True)
            for k in range(tiles):
                ks = slice(k * T, (k + 1) * T)
                for i in range(k, tiles):
                    cols = slice(i * T, (i + 1) * T)
                    ref, a, b = ef(k, i)
                    dp = dot(vn[n, ks, :], do[:, cols]) - delta[:, cols]
                    ds[ks, cols] = (ref[h, a : a + T, b : b + T].astype(F32) * dp).astype(BF16)
                ref, a, b = ef(k, k)
                dv[ks, :] += dot_t(ref[h, a : a + T, b : b + rows - k * T], do[:, k * T :])
                dk[ks, :] += dot_t(ds[ks, k * T :], qt[h, :, k * T :])
            dq = [
                dot(kt_[n, :, : (i + 1) * T], ds[: (i + 1) * T, i * T : (i + 1) * T])
                for i in range(tiles)
            ]
            unrotate(jnp.concatenate(dq, axis=1) * (HS**-0.5), h * HS)

            @pl.when(lax.rem(h, GROUP) == GROUP - 1)
            def _():
                unrotate(dk[...].T, H * HS + n * HS)
                gjt[pl.ds(pl.multiple_of((H + KV + n) * HS, HS), HS), :] = dv[...].T.astype(BF16)

            return 0

        lax.fori_loop(0, H, head, 0)

        for p in range(2):
            part = dot_t(nt[...], gjt[p * PC : (p + 1) * PC, :]).astype(BF16)
            gr_ref[3, :, p] = part.reshape(4, PR, PC)
        part = dot_t(nt[...], gjt[2 * PC :, :]).astype(BF16)
        gr_ref[3, :, 2, :, : PC // 2] = part.reshape(4, PR, PC // 2)

        def rowtile(r, _):
            rs = pl.ds(pl.multiple_of(r * T, T), T)
            gn = dot(wp_ref[...], gjt[:, rs])
            unit, scale = unit_one(rs)
            dgain[:, 0:1] += jnp.sum(gn * unit, axis=1, keepdims=True)
            e = gn * gain1
            tg = gres[:, rs] + scale * (e - unit * jnp.mean(e * unit, axis=0, keepdims=True))
            tgt_ref[:, rs] = tg.astype(BF16)
            return 0

        lax.fori_loop(0, rows // T, rowtile, 0)
        for s in range(4):
            gain_ref[s] = dgain[s * PR : (s + 1) * PR, :].T

    pl.run_scoped(
        backward,
        pltpu.VMEM((rows, rows), BF16),
        pltpu.VMEM((QKV, rows), BF16),
        pltpu.VMEM((rows, HS), F32),
        pltpu.VMEM((rows, HS), F32),
        pltpu.VMEM((half, rows), F32),
        pltpu.VMEM((half, rows), F32),
    )


def run_block(xt, ct, seg, g1, g2, wp, wo, wg, wu, wdt):
    rows = xt.shape[1]
    vm = pl.BlockSpec(memory_space=pltpu.VMEM)
    sd = jax.ShapeDtypeStruct
    return pl.pallas_call(
        block_kernel,
        name="block",
        out_shape=(
            sd((D, rows), BF16),
            sd((D, rows), BF16),
            sd((4, 8, PR), F32),
            sd((4, 4, 4, PR, PC), BF16),
        ),
        in_specs=[vm] * 10,
        out_specs=(vm,) * 4,
        scratch_shapes=[
            pltpu.VMEM((H, HS, rows), BF16),
            pltpu.VMEM((KV, HS, rows), BF16),
            pltpu.VMEM((KV, HS, rows), BF16),
            pltpu.VMEM((KV, rows, HS), BF16),
            pltpu.VMEM((KV, rows, HS), BF16),
            pltpu.VMEM((D, rows), BF16),
            pltpu.VMEM((D, rows), BF16),
            pltpu.VMEM((D, rows), BF16),
            pltpu.VMEM((H, 2 * T, rows), BF16),
            pltpu.VMEM((H, 2 * T, rows - 2 * T), BF16),
            pltpu.VMEM((H, 1, rows), F32),
            pltpu.VMEM((D, rows), F32),
            pltpu.VMEM((D, 8), F32),
        ],
        compiler_params=pltpu.CompilerParams(vmem_limit_bytes=62 * 2**20),
    )(xt, ct, seg.reshape(1, rows), g1, g2, wp, wo, wg, wu, wdt)
MESH = pl.DeviceIdType.MESH
SPLIT = 80
RATES = tuple(
    BASE_RATE * v
    for v in (float(D) ** -0.5, float(D) ** -0.5, float(FF) ** -0.5, float(D) ** -0.5, float(max(D // 96, 1)) ** -0.5)
)
CORRECTION = 1.0 - BETA**STEP


def adam(grad, master, moment, variance, rate, decay):
    velocity = BETA * moment + (1.0 - BETA) * grad
    spread = BETA * variance + (1.0 - BETA) * grad * grad
    direction = velocity / CORRECTION / (jnp.sqrt(spread / CORRECTION) + ADAM_EPSILON)
    if decay:
        direction = direction + DECAY * master
    return velocity, spread, master - rate * direction


def places(t, p):
    if t < 2:
        return [(0, t, 0, p * PC, PR, PC)]
    if t == 2:
        return [(0, 2, p * PR, 0, PR, PC)]
    if p < 2:
        return [(0, 3, 0, p * PC, PR, PC)]
    if p == 2:
        return [(0, 3, 0, 2 * PC, PR, PC // 2), (PC // 2, 4, 0, PC, PR, PC // 2)]
    return [(0, 4, 0, 0, PR, PC)]


def add_into(dst, a, b):
    dst[...] = (a[...].astype(F32) + b[...].astype(F32)).astype(BF16)


def exchange_kernel(bits, total, *refs):
    gr_ref, gain_ref = refs[:2]
    state = refs[2:17]
    gain_state = refs[17:23]
    gf_ref, u_ref, gsum_ref, gup_ref = refs[23:27]
    (s1, r1, s2a, r2a, s2b, r2b, s3, r3, s4, r4, r5, s5, up, gs, grc, gu) = refs[27:43]
    held = refs[43:58]
    send_sem, recv_sem, load_sem, keep_sem = refs[58:62]

    shard = lax.axis_index("shard")
    rep = lax.axis_index("rep")
    x, core = shard // 2, lax.rem(shard, 2)
    y, zl = lax.rem(rep, 2), lax.rem(rep // 2, 2)

    def flip(index, bit):
        size = 1 << bit
        return index + size - 2 * size * lax.rem(index // size, 2)

    peer_c = (flip(shard, 0), rep)
    peer_x = (flip(shard, 1), rep)
    peer_r = [(shard, flip(rep, b)) for b in range(bits)]
    peers = [peer_c, peer_x] + peer_r

    loads = []
    for number in range(15):
        loads.append(pltpu.make_async_copy(state[number], held[number], load_sem.at[number]))
        loads[-1].start()

    barrier = pltpu.get_barrier_semaphore()
    for peer in peers:
        pl.semaphore_signal(barrier, inc=1, device_id=peer, device_id_type=MESH)
    pl.semaphore_wait(barrier, len(peers))

    sent = []

    def send(src, dst, peer):
        n = len(sent)
        copy = pltpu.make_async_remote_copy(
            src_ref=src, dst_ref=dst, send_sem=send_sem.at[n], recv_sem=recv_sem.at[n],
            device_id=peer, device_id_type=MESH,
        )
        copy.start()
        sent.append(copy)
        return copy

    keeps = []

    def gain_flow():
        copy = send(gain_ref, grc.at[0], peer_c)
        yield
        for b, peer in enumerate(peers):
            copy.wait_recv()
            gs[b] = (gain_ref[...] if b == 0 else gs[b - 1]) + grc[b]
            if b + 1 < len(peers):
                copy = send(gs.at[b], grc.at[b + 1], peers[b + 1])
                yield
        gsum_ref[...] = gs[len(peers) - 1]
        grad = gs[len(peers) - 1, shard] / total
        for k in range(2):
            m, v, w = (gain_state[2 * q + k][...].reshape(1, PR) for q in range(3))
            gu[shard, k : k + 1, :] = adam(grad[k : k + 1], m, v, w, BASE_RATE, False)[2]
        copy = send(gu.at[shard], gu.at[shard], peer_x)
        yield
        copy.wait_recv()
        one = send(gu.at[shard], gu.at[shard], peer_c)
        two = send(gu.at[flip(shard, 1)], gu.at[flip(shard, 1)], peer_c)
        yield
        one.wait_recv()
        two.wait_recv()
        gup_ref[...] = gu[...]

    def flow(t):
        copies = [
            send(gr_ref.at[t, 2 * i + 1 - core], r1.at[t, i], peer_c) for i in range(2)
        ]
        yield
        for copy in copies:
            copy.wait_recv()
        for i in range(2):
            def step(p, _):
                add_into(s1.at[t, i, p], gr_ref.at[t, 2 * i + core, p], r1.at[t, i, p])
                return 0

            lax.fori_loop(0, 4, step, 0)
        a, b = pl.ds(0, SPLIT), pl.ds(SPLIT, PR - SPLIT)
        one = send(s1.at[t, 1 - x, :, a], r2a.at[t], peer_x)
        two = send(s1.at[t, :, pl.ds(2 * (1 - y), 2), b], r2b.at[t], peer_r[0])
        yield
        one.wait_recv()
        two.wait_recv()
        for p in range(4):
            add_into(s2a.at[t, p], s1.at[t, x, p, a], r2a.at[t, p])
        for i in range(2):
            for q in range(2):
                add_into(s2b.at[t, i, q], s1.at[t, i, 2 * y + q, b], r2b.at[t, i, q])
        one = send(s2a.at[t, pl.ds(2 * (1 - y), 2)], r3.at[t, :, a], peer_r[0])
        two = send(s2b.at[t, 1 - x], r3.at[t, :, b], peer_x)
        yield
        one.wait_recv()
        two.wait_recv()
        for q in range(2):
            add_into(s3.at[t, q, a], s2a.at[t, 2 * y + q], r3.at[t, q, a])
            add_into(s3.at[t, q, b], s2b.at[t, x, q], r3.at[t, q, b])
        copy = send(s3.at[t, 1 - zl], r4.at[t], peer_r[1])
        yield
        copy.wait_recv()
        add_into(s4.at[t, 0], s3.at[t, zl], r4.at[t])
        for k in range(bits - 2):
            copy = send(s4.at[t, k], r5.at[t, k], peer_r[2 + k])
            yield
            copy.wait_recv()
            add_into(s4.at[t, k + 1], s4.at[t, k], r5.at[t, k])
        mine = 2 * y + zl
        s5[t, mine] = s4[t, bits - 2]
        copy = send(s4.at[t, bits - 2], s5.at[t, mine], peer_r[1])
        yield
        copy.wait_recv()
        copy = send(s5.at[t, pl.ds(2 * y, 2)], s5.at[t, pl.ds(2 * y, 2)], peer_r[0])
        yield
        copy.wait_recv()
        keeps.append(pltpu.make_async_copy(s5.at[t], gf_ref.at[t], keep_sem.at[2 * t]))
        keeps[-1].start()
        numbers = (3, 4) if t == 3 else (t,)
        for number in numbers:
            for k in range(3):
                loads[5 * k + number].wait()
        for p in range(4):
            for col, number, r0, c0, nr, nc in places(t, p):
                where = (slice(r0, r0 + nr), slice(c0, c0 + nc))
                m, v, w = (held[5 * k + number][where] for k in range(3))
                grad = s5[t, p, :, col : col + nc].astype(F32) / total
                up[t, p, :, col : col + nc] = adam(grad, m, v, w, RATES[number], True)[2].astype(BF16)
        copy = send(up.at[t], u_ref.at[t, shard], peer_x)
        keeps.append(pltpu.make_async_copy(up.at[t], u_ref.at[t, shard], keep_sem.at[2 * t + 1]))
        keeps[-1].start()
        one = send(up.at[t], u_ref.at[t, shard], peer_c)
        yield
        copy.wait_recv()
        other = flip(shard, 1)
        two = send(u_ref.at[t, other], u_ref.at[t, other], peer_c)
        yield
        one.wait_recv()
        two.wait_recv()

    flows = [gain_flow()] + [flow(t) for t in range(4)]
    offsets = [0, 0, 1, 2, 3]
    slot = 0
    live = set(range(5))
    while live:
        for k in range(5):
            if k in live and slot >= offsets[k]:
                try:
                    next(flows[k])
                except StopIteration:
                    live.discard(k)
        slot += 1
    for copy in sent:
        copy.wait_send()
    for copy in keeps:
        copy.wait()


def run_exchange(mesh_shape, rows, gr, gains, state, gain_state):
    bits = mesh_shape["rep"].bit_length() - 1
    total = float(rows * mesh_shape["rep"] * mesh_shape["shard"])
    vm = pl.BlockSpec(memory_space=pltpu.VMEM)
    hbm = pl.BlockSpec(memory_space=pl.ANY)
    sd = jax.ShapeDtypeStruct
    copies = 4 * (9 + bits) + (bits + 2) + 3 + 8
    npeer = bits + 2
    return pl.pallas_call(
        lambda *refs: exchange_kernel(bits, total, *refs),
        name="exchange",
        out_shape=(
            sd((4, 4, PR, PC), BF16),
            sd((4, 4, 4, PR, PC), BF16),
            sd((4, 8, PR), F32),
            sd((4, 8, PR), F32),
        ),
        in_specs=[vm, vm] + [hbm] * 15 + [vm] * 6,
        out_specs=(hbm, hbm, vm, vm),
        scratch_shapes=[
            pltpu.VMEM((4, 2, 4, PR, PC), BF16),
            pltpu.VMEM((4, 2, 4, PR, PC), BF16),
            pltpu.VMEM((4, 4, SPLIT, PC), BF16),
            pltpu.VMEM((4, 4, SPLIT, PC), BF16),
            pltpu.VMEM((4, 2, 2, PR - SPLIT, PC), BF16),
            pltpu.VMEM((4, 2, 2, PR - SPLIT, PC), BF16),
            pltpu.VMEM((4, 2, PR, PC), BF16),
            pltpu.VMEM((4, 2, PR, PC), BF16),
            pltpu.VMEM((4, bits - 1, PR, PC), BF16),
            pltpu.VMEM((4, PR, PC), BF16),
            pltpu.VMEM((4, bits - 2, PR, PC), BF16),
            pltpu.VMEM((4, 4, PR, PC), BF16),
            pltpu.VMEM((4, 4, PR, PC), BF16),
            pltpu.VMEM((npeer, 4, 8, PR), F32),
            pltpu.VMEM((npeer, 4, 8, PR), F32),
            pltpu.VMEM((4, 8, PR), F32),
        ]
        + [pltpu.VMEM(a.shape, F32) for a in state]
        + [
            pltpu.SemaphoreType.DMA((copies,)),
            pltpu.SemaphoreType.DMA((copies,)),
            pltpu.SemaphoreType.DMA((15,)),
            pltpu.SemaphoreType.DMA((8,)),
        ],
        compiler_params=pltpu.CompilerParams(
            vmem_limit_bytes=62 * 2**20, collective_id=0, has_side_effects=True
        ),
    )(gr, gains, *state, *gain_state)


def update_kernel(total, *refs):
    gf_ref, u_ref, gsum_ref = refs[:3]
    state = refs[3:18]
    gain_state = refs[18:24]
    outs = refs[24:44]
    gain_outs = refs[44:52]
    rounded = refs[52:57]
    low, sem = refs[57:]
    copies = []
    for t in range(3):
        for s in range(4):
            for p in range(4):
                a, b = (s, p) if t < 2 else (p, s)
                dst = rounded[t].at[pl.ds(a * PR, PR), pl.ds(b * PC, PC)]
                copies.append(pltpu.make_async_copy(u_ref.at[t, s, p], dst, sem.at[len(copies)]))
    copies.append(pltpu.make_async_copy(u_ref.at[3], low, sem.at[len(copies)]))
    for copy in copies:
        copy.start()
    shard = lax.axis_index("shard")
    grad = gsum_ref[shard] / total
    for k in range(2):
        m, v, w = (gain_state[2 * q + k][...].reshape(1, PR) for q in range(3))
        one = grad[k : k + 1]
        velocity, spread, updated = adam(one, m, v, w, BASE_RATE, False)
        for q, value in enumerate((one, updated, velocity, spread)):
            gain_outs[2 * q + k][...] = value.reshape(PR)
    for t in range(4):
        for p in range(4):
            for col, number, r0, c0, nr, nc in places(t, p):
                where = (slice(r0, r0 + nr), slice(c0, c0 + nc))
                m, v, w = (state[5 * k + number][where] for k in range(3))
                grad = gf_ref[t, p, :, col : col + nc].astype(F32) / total
                velocity, spread, updated = adam(grad, m, v, w, RATES[number], True)
                for q, value in enumerate((grad, updated, velocity, spread)):
                    outs[5 * q + number][where] = value
    copies[-1].wait()
    for s in range(4):
        for p in range(4):
            for col, number, r0, c0, nr, nc in places(3, p):
                rounded[number][s * PR : (s + 1) * PR, c0 : c0 + nc] = low[s, p, :, col : col + nc]
    for copy in copies[:-1]:
        copy.wait()


def run_update(total, gf, u, gsum, state, gain_state):
    vm = pl.BlockSpec(memory_space=pltpu.VMEM)
    hbm = pl.BlockSpec(memory_space=pl.ANY)
    sd = jax.ShapeDtypeStruct
    shapes = [a.shape for a in state[:5]]
    return pl.pallas_call(
        lambda *refs: update_kernel(total, *refs),
        name="update",
        out_shape=tuple(sd(s, F32) for s in shapes * 4)
        + (sd((PR,), F32),) * 8
        + (sd((D, FF), BF16),) * 3
        + (sd((D, QKV), BF16), sd((D, D), BF16)),
        in_specs=[vm, hbm, vm] + [vm] * 21,
        out_specs=(vm,) * 28 + (hbm,) * 3 + (vm,) * 2,
        scratch_shapes=[pltpu.VMEM((4, 4, PR, PC), BF16), pltpu.SemaphoreType.DMA((49,))],
        compiler_params=pltpu.CompilerParams(vmem_limit_bytes=62 * 2**20),
    )(gf, u, gsum, *state, *gain_state)


def solution(mesh):
    mesh_shape = dict(mesh.shape)

    def body(
        tokens, cotangent, segment_ids, current_attention, current_project, current_output,
        current_feeding, current_gating, current_upward, current_downward, *state_all,
    ):
        rows = tokens.shape[0]
        total = float(rows * mesh_shape["rep"] * mesh_shape["shard"])
        state, gain_state = [], []
        for k in range(3):
            at, pr, ou, fe, ga, uw, dw = state_all[7 * k : 7 * k + 7]
            state += [ga, uw, dw.T, pr, ou]
            gain_state += [at, fe]
        bot, tgt, gains, gr = run_block(
            tokens.T, cotangent.T, segment_ids, current_attention, current_feeding,
            current_project, current_output, current_gating, current_upward, current_downward.T,
        )
        gf, u, gsum, gup = run_exchange(mesh_shape, rows, gr, gains, state, gain_state)
        out = run_update(total, gf, u, gsum, state, gain_state)
        results = [bot.T, tgt.T]
        for q in range(4):
            ga, uw, dw, pr, ou = out[5 * q : 5 * q + 5]
            at, fe = out[20 + 2 * q : 22 + 2 * q]
            results += [at, pr, ou, fe, ga, uw, dw.T]
        ga, uw, dw, pr, ou = out[28:33]
        at, fe = (gup[:, k].reshape(D).astype(BF16) for k in range(2))
        return (*results, at, pr, ou, fe, ga, uw, dw.T)

    row, vec = P("shard", None), P("shard")
    seven = (vec, row, row, vec, row, row, row)
    spread = P(("shard", "rep"), None)
    in_specs = (spread, spread, P(("shard", "rep"))) + (P(),) * 7 + seven * 3
    out_specs = (spread, spread) + seven * 4 + (P(),) * 7
    return jax.shard_map(body, mesh=mesh, in_specs=in_specs, out_specs=out_specs, check_vma=False)
```

time: 545 us -> 349 us (0.64); the launches traced: 538 us -> 349 us
  Pallas kernels: 0 us -> 346 us
  waiting for transfers between devices: 259 us -> 0 us
  matrix products: 113 us -> 0 us
  other arithmetic: 68.8 us -> 0.76 us
  blocking collectives: 59.5 us -> 0 us
  local copies, waits for them, and re-layouts: 21.4 us -> 1.37 us
  between operations: 16.4 us -> 0.88 us
    pallas_call x0 -> x3, Pallas kernels: none -> 346 us  [the longest x1 173 us: run_update(): pl.pallas_call(lambda *refs: update_kernel(total, *refs), name='update',...]
    psum x1 -> x0, waiting for transfers between devices: 259 us -> none  [body(): lax.psum((grad_attention, grad_project, grad_output, grad_feeding, grad_g...]
    dot_general x27 -> x0, matrix products: 113 us -> none  [the longest x5 19 us: back_product(): lax.dot_general(left, right, (((1,), (1,)), ((), ())), preferred_element_...]
    convert_element_type x13 -> x0, other arithmetic: 50 us -> none  [the longest x2 25.1 us: body(): grad_scores = (probability * (grad_weights - centre)).astype(jnp.bfloat16)]
    psum x1 -> x0, blocking collectives: 39.7 us -> none  [body(): lax.psum((grad_attention, grad_project, grad_output, grad_feeding, grad_g...]
    unnamed x128 -> x0, local copies, waits for them, and re-layouts: 15.8 us -> none
    reduce_sum x3 -> x0, other arithmetic: 13.7 us -> none  [the longest x2 12.1 us: body(): row_total = jnp.sum(exponents, axis=-1, keepdims=True)]
    all_gather x1 -> x0, blocking collectives: 12.6 us -> none  [body(): lax.all_gather(updates[2].astype(jnp.bfloat16), 'shard', axis=0, tiled=True)]
  transfers between devices with their start and end apart: 5 -> 0, of which waited for: 2 -> 0; matrix products, arithmetic and copies ran while one was open for 5% -> 0% of each run, Pallas kernels for 0% -> 0%
where the time goes in v1:
time: 349 us
  Pallas kernels  346 us (99%)
    pallas_call x1, Pallas kernels, run_update(): pl.pallas_call(lambda *refs: update_kernel(total, *refs), name='update',...  173 us
    pallas_call x1, Pallas kernels, run_exchange(): pl.pallas_call(lambda *refs: exchange_kernel(bits, total, *refs), name='e...  96 us
    pallas_call x1, Pallas kernels, run_block(): pl.pallas_call(block_kernel, name='block', out_shape=(sd((D, rows), BF16)...  76.9 us

profile of v1, /device:TPU:1, one launch (start us, length us, event | category | flops | bytes accessed | tf_op | source)
XLA Modules:
  0.0 348.5 jit_solution(17087878801140277667)
XLA Ops:
  0.7 76.9 %block.1 = (bf16[576,1024]{1,0:T(8,128)(2,1)}, bf16[576,1024]{1,0:T(8,128)(2,1)}, f32[4,8,144]{2,1,0:T(8,128)}, bf16[4,4,4,144,384]{4,3,2,1,0:T(8,128)(2,1)}) custom-call(bf16[576,1024]{1,0:T(8,128)(2,1)} %bitcast.21, bf16[576,1024]{1,0:T(8,128)(2,1)} %bitcast.22, s32[1,1024]{1,0:T(1,128)} %bitcast.23, bf16[576]{0:T(1024)(128)(2,1)} %g1_ref.1, ...), custom_call_target="tpu_custom_call" | custom-call | tf_op jit(solution)/shard_map/block/pallas_call | solution.py:307
  77.6 96.0 %exchange.1 = (bf16[4,4,144,384]{3,2,1,0:T(8,128)(2,1)}, bf16[4,4,4,144,384]{4,3,2,1,0:T(8,128)(2,1)}, f32[4,8,144]{2,1,0:T(8,128)}, f32[4,8,144]{2,1,0:T(8,128)}) custom-call(bf16[4,4,4,144,384]{4,3,2,1,0:T(8,128)(2,1)} %get-tuple-element.80.refs_0_, f32[4,8,144]{2,1,0:T(8,128)} %get-tuple-element.81.refs_1_, f32[144,1536]{1,0:T(8,128)} %refs_3_.3, ...), custom_call_target="tpu_custom_call" | custom-call | tf_op jit(solution)/shard_map/exchange/pallas_call | solution.py:539
  173.5 0.8 convert.4
  174.3 0.7 convert_element_type.9
  175.0 0.7 convert_element_type.8
  175.7 172.7 %update.1 = (f32[144,1536]{1,0:T(8,128)}, f32[144,1536]{1,0:T(8,128)}, f32[576,384]{1,0:T(8,128)}, f32[144,960]{1,0:T(8,128)}, f32[144,576]{1,0:T(8,128)}, /*ind...) custom-call(bf16[4,4,144,384]{3,2,1,0:T(8,128)(2,1)} %get-tuple-elem, ...), custom_call_target="tpu_custom_call" | custom-call | tf_op jit(solution)/shard_map/update/pallas_call | solution.py:630
  (1 shorter events, 0.0 us)

commit v2 on v1

--- a/solution.py
+++ b/solution.py
@@ -499,9 +499,8 @@
                 grad = s5[t, p, :, col : col + nc].astype(F32) / total
                 up[t, p, :, col : col + nc] = adam(grad, m, v, w, RATES[number], True)[2].astype(BF16)
         copy = send(up.at[t], u_ref.at[t, shard], peer_x)
-        keeps.append(pltpu.make_async_copy(up.at[t], u_ref.at[t, shard], keep_sem.at[2 * t + 1]))
-        keeps[-1].start()
         one = send(up.at[t], u_ref.at[t, shard], peer_c)
+        u_ref[t, shard] = up[t]
         yield
         copy.wait_recv()
         other = flip(shard, 1)
@@ -546,7 +545,7 @@
             sd((4, 8, PR), F32),
         ),
         in_specs=[vm, vm] + [hbm] * 15 + [vm] * 6,
-        out_specs=(hbm, hbm, vm, vm),
+        out_specs=(hbm, vm, vm, vm),
         scratch_shapes=[
             pltpu.VMEM((4, 2, 4, PR, PC), BF16),
             pltpu.VMEM((4, 2, 4, PR, PC), BF16),
@@ -585,17 +584,33 @@
     outs = refs[24:44]
     gain_outs = refs[44:52]
     rounded = refs[52:57]
-    low, sem = refs[57:]
-    copies = []
-    for t in range(3):
-        for s in range(4):
-            for p in range(4):
-                a, b = (s, p) if t < 2 else (p, s)
-                dst = rounded[t].at[pl.ds(a * PR, PR), pl.ds(b * PC, PC)]
-                copies.append(pltpu.make_async_copy(u_ref.at[t, s, p], dst, sem.at[len(copies)]))
-    copies.append(pltpu.make_async_copy(u_ref.at[3], low, sem.at[len(copies)]))
-    for copy in copies:
-        copy.start()
+    gf, low = refs[57:59]
+    held = refs[59:74]
+    made = refs[74:94]
+    wide = refs[94:99]
+    load_sem, low_sem, gf_sem, out_sem, wide_sem = refs[99:]
+
+    order = (0, 1, 2, 3, 4)
+    loads = {}
+    grads = []
+    for t in range(4):
+        grads.append(pltpu.make_async_copy(gf_ref.at[t], gf.at[t], gf_sem.at[t]))
+        grads[-1].start()
+        for number in ((t,) if t < 3 else (3, 4)):
+            for k in range(3):
+                n = 5 * k + number
+                loads[n] = pltpu.make_async_copy(state[n], held[n], load_sem.at[n])
+                loads[n].start()
+    lows = []
+    for t in range(4):
+        lows.append(pltpu.make_async_copy(u_ref.at[t], low.at[t], low_sem.at[t]))
+        lows[-1].start()
+    stores = []
+
+    def store(src, dst, sem):
+        stores.append(pltpu.make_async_copy(src, dst, sem))
+        stores[-1].start()
+
     shard = lax.axis_index("shard")
     grad = gsum_ref[shard] / total
     for k in range(2):
@@ -605,20 +620,34 @@
         for q, value in enumerate((one, updated, velocity, spread)):
             gain_outs[2 * q + k][...] = value.reshape(PR)
     for t in range(4):
+        numbers = (t,) if t < 3 else (3, 4)
+        grads[t].wait()
+        for number in numbers:
+            for k in range(3):
+                loads[5 * k + number].wait()
         for p in range(4):
             for col, number, r0, c0, nr, nc in places(t, p):
                 where = (slice(r0, r0 + nr), slice(c0, c0 + nc))
-                m, v, w = (state[5 * k + number][where] for k in range(3))
-                grad = gf_ref[t, p, :, col : col + nc].astype(F32) / total
+                m, v, w = (held[5 * k + number][where] for k in range(3))
+                grad = gf[t, p, :, col : col + nc].astype(F32) / total
                 velocity, spread, updated = adam(grad, m, v, w, RATES[number], True)
                 for q, value in enumerate((grad, updated, velocity, spread)):
-                    outs[5 * q + number][where] = value
-    copies[-1].wait()
-    for s in range(4):
-        for p in range(4):
-            for col, number, r0, c0, nr, nc in places(3, p):
-                rounded[number][s * PR : (s + 1) * PR, c0 : c0 + nc] = low[s, p, :, col : col + nc]
-    for copy in copies[:-1]:
+                    made[5 * q + number][where] = value
+        for number in numbers:
+            for q in range(4):
+                n = 5 * q + number
+                store(made[n], outs[n], out_sem.at[n])
+        lows[t].wait()
+        for s in range(4):
+            for p in range(4):
+                if t == 2:
+                    wide[2][p * PR : (p + 1) * PR, s * PC : (s + 1) * PC] = low[2, s, p]
+                    continue
+                for col, number, r0, c0, nr, nc in places(t, p):
+                    wide[number][s * PR : (s + 1) * PR, c0 : c0 + nc] = low[t, s, p, :, col : col + nc]
+        for number in numbers:
+            store(wide[number], rounded[number], wide_sem.at[number])
+    for copy in stores:
         copy.wait()
 
 
@@ -627,16 +656,23 @@
     hbm = pl.BlockSpec(memory_space=pl.ANY)
     sd = jax.ShapeDtypeStruct
     shapes = [a.shape for a in state[:5]]
+    full = [(D, FF)] * 3 + [(D, QKV), (D, D)]
     return pl.pallas_call(
         lambda *refs: update_kernel(total, *refs),
         name="update",
         out_shape=tuple(sd(s, F32) for s in shapes * 4)
         + (sd((PR,), F32),) * 8
-        + (sd((D, FF), BF16),) * 3
-        + (sd((D, QKV), BF16), sd((D, D), BF16)),
-        in_specs=[vm, hbm, vm] + [vm] * 21,
-        out_specs=(vm,) * 28 + (hbm,) * 3 + (vm,) * 2,
-        scratch_shapes=[pltpu.VMEM((4, 4, PR, PC), BF16), pltpu.SemaphoreType.DMA((49,))],
+        + tuple(sd(s, BF16) for s in full),
+        in_specs=[hbm, hbm, vm] + [hbm] * 15 + [vm] * 6,
+        out_specs=(hbm,) * 20 + (vm,) * 8 + (hbm,) * 5,
+        scratch_shapes=[
+            pltpu.VMEM((4, 4, PR, PC), BF16),
+            pltpu.VMEM((4, 4, 4, PR, PC), BF16),
+        ]
+        + [pltpu.VMEM(s, F32) for s in shapes * 3]
+        + [pltpu.VMEM(s, F32) for s in shapes * 4]
+        + [pltpu.VMEM(s, BF16) for s in full]
+        + [pltpu.SemaphoreType.DMA((n,)) for n in (15, 4, 4, 20, 5)],
         compiler_params=pltpu.CompilerParams(vmem_limit_bytes=62 * 2**20),
     )(gf, u, gsum, *state, *gain_state)
 

time: 349 us -> 192 us (0.55)
  Pallas kernels: 346 us -> 189 us
    pallas_call x1, Pallas kernels: 173 us -> 14.5 us  [run_update(): pl.pallas_call(lambda *refs: update_kernel(total, *refs), name='update',...]
where the time goes in v2:
time: 192 us
  Pallas kernels  189 us (98%)
    pallas_call x1, Pallas kernels, run_exchange(): pl.pallas_call(lambda *refs: exchange_kernel(bits, total, *refs), name='e...  97.3 us
    pallas_call x1, Pallas kernels, run_block(): pl.pallas_call(block_kernel, name='block', out_shape=(sd((D, rows), BF16)...  76.9 us
    pallas_call x1, Pallas kernels, run_update(): pl.pallas_call(lambda *refs: update_kernel(total, *refs), name='update',...  14.5 us

profile of v2, /device:TPU:1, one launch (start us, length us, event | category | flops | bytes accessed | tf_op | source)
XLA Modules:
  0.0 191.7 jit_solution(5529237233009803590)
XLA Ops:
  0.7 76.9 %block.1 = (bf16[576,1024]{1,0:T(8,128)(2,1)}, bf16[576,1024]{1,0:T(8,128)(2,1)}, f32[4,8,144]{2,1,0:T(8,128)}, bf16[4,4,4,144,384]{4,3,2,1,0:T(8,128)(2,1)}) custom-call(bf16[576,1024]{1,0:T(8,128)(2,1)} %bitcast.21, bf16[576,1024]{1,0:T(8,128)(2,1)} %bitcast.22, s32[1,1024]{1,0:T(1,128)} %bitcast.23, bf16[576]{0:T(1024)(128)(2,1)} %g1_ref.1, ...), custom_call_target="tpu_custom_call" | custom-call | tf_op jit(solution)/shard_map/block/pallas_call | solution.py:307
  77.6 97.3 %exchange.1 = (bf16[4,4,144,384]{3,2,1,0:T(8,128)(2,1)}, bf16[4,4,4,144,384]{4,3,2,1,0:T(8,128)(2,1)}, f32[4,8,144]{2,1,0:T(8,128)}, f32[4,8,144]{2,1,0:T(8,128)}) custom-call(bf16[4,4,4,144,384]{4,3,2,1,0:T(8,128)(2,1)} %get-tuple-element.80.refs_0_, f32[4,8,144]{2,1,0:T(8,128)} %get-tuple-element.81.refs_1_, f32[144,1536]{1,0:T(8,128)} %refs_3_.3, ...), custom_call_target="tpu_custom_call" | custom-call | tf_op jit(solution)/shard_map/exchange/pallas_call | solution.py:538
  174.9 0.8 convert.4
  175.7 0.7 convert_element_type.9
  176.4 0.7 convert_element_type.8
  177.0 14.5 %update.1 = (f32[144,1536]{1,0:T(8,128)}, f32[144,1536]{1,0:T(8,128)}, f32[576,384]{1,0:T(8,128)}, f32[144,960]{1,0:T(8,128)}, f32[144,576]{1,0:T(8,128)}, /*ind...) custom-call(bf16[4,4,144,384]{3,2,1,0:T(8,128)(2,1)} %get-tuple-elem, ...), custom_call_target="tpu_custom_call" | custom-call | tf_op jit(solution)/shard_map/update/pallas_call | solution.py:660
  (1 shorter events, 0.0 us)
